TPU v7x, 256 devices: a whole 4x4x8 slice. The times are simulated.
256 devices in a mesh: depth: 128 (over x, y, z_lo, core), lat: 2 (over z_hi).
Axes of the slice: x: 4, y: 4, z: 8 (z_hi: 2, z_lo: 4; z = z_hi * 4 + z_lo), core: 2. Of those that a mesh axis runs over, the one named last changes fastest.
Arguments:
- sources: float32 [128, 16, 6144], P('depth', None, 'lat'), may hold values from -6 to 6
- frontal: bfloat16 [128, 48, 8, 128, 128], P('depth', 'lat'), may hold values from -0.1875 to 0.1875
- couplings: bfloat16 [128, 2, 48, 2, 128, 128], P('depth', None, 'lat'), may hold values from -0.375 to 0.375
- pattern: int32 [128, 48, 8], P('depth', 'lat'), may hold values from 0 to 47, as said below
Outputs:
- swept: float32 [128, 16, 6144], P('depth', None, 'lat')
Inputs may be any that keep to these rules, and one draw needn't show every extreme that they name: Entry 0 of pattern[p, r] is r itself; the other entries of a block row differ from r and from each other.
All inputs are finite; a program needn't handle non-finite values.
Results may differ from a plain program's by a relative error of at most 0.035.
Values may be sent and summed in bfloat16 or wider, within the bound.
A program may use at most 128 MiB of HBM per device.

v0:
```python
import jax
import jax.numpy as jnp
from jax import lax
from jax.sharding import PartitionSpec as P

BLK = 128
KC = 2
SEG = 8
NBR = 48


def shifted(block, axis, distance):
    devices = range(lax.axis_size(axis))
    route = [(i - distance, i) for i in devices if i - distance in devices]
    return lax.ppermute(block, axis, route)


def apply_blocks(blocks, cols, vector):
    shots = vector.shape[0]
    block = blocks.shape[-1]
    grouped = vector.reshape(shots, vector.shape[1] // block, block)
    picked = grouped[:, cols]
    result = jnp.einsum("rkij,srkj->sri", blocks, picked, preferred_element_type=jnp.float32)
    return result.reshape(shots, blocks.shape[0] * block)


def planes(vector):
    return lax.all_gather(vector, "lat", axis=1, tiled=True)


def half_planes(vector):
    return lax.all_gather(vector, "lat", axis=1, tiled=True)


def local(sources, frontal, couplings, pattern):
    mine = lax.axis_index("depth")
    place = mine % SEG
    src_all = sources[0]
    factor = frontal[0]
    cols = pattern[0]
    couple_cols = cols[:, :KC]
    ahead_coupling = couplings[0, 0]
    behind_coupling = couplings[0, 1]
    shots = src_all.shape[0]
    couple_unk = ahead_coupling.shape[0] * BLK
    field_unk = factor.shape[0] * BLK
    whole_unk = NBR * BLK
    groups = 1
    width = shots // groups
    nothing = jnp.zeros((width, field_unk), jnp.float32)
    no_couple = jnp.zeros((width, couple_unk), jnp.float32)

    def send_out(vector):
        return planes(vector)

    def forward_step(turn, carry):
        outgoing, store = carry
        incoming = shifted(outgoing, "depth", 1)
        incoming = jnp.where(place == 0, jnp.zeros_like(incoming), incoming)
        slot = turn - place
        valid = jnp.logical_and(slot >= 0, slot < groups)
        slot = jnp.clip(slot, 0, groups - 1)
        coupled = lax.cond(
            valid, lambda: apply_blocks(ahead_coupling, couple_cols, incoming), lambda: no_couple
        )
        reduced = (src_all - coupled).astype(jnp.bfloat16)
        reduced = half_planes(reduced)
        field = lax.cond(valid, lambda: apply_blocks(factor, cols, reduced), lambda: nothing)
        store = jnp.where(valid, field, store)
        outgoing = send_out(field.astype(jnp.bfloat16))
        return (outgoing, store)

    empty_send = jnp.zeros((width, whole_unk), jnp.bfloat16)
    empty_store = jnp.zeros((shots, field_unk), jnp.float32)
    _, forward = lax.fori_loop(0, SEG + groups - 1, forward_step, (empty_send, empty_store))

    def backward_step(turn, carry):
        outgoing, store = carry
        incoming = shifted(outgoing, "depth", -1)
        incoming = jnp.where(place == SEG - 1, jnp.zeros_like(incoming), incoming)
        slot = turn - (SEG - 1 - place)
        valid = jnp.logical_and(slot >= 0, slot < groups)
        slot = jnp.clip(slot, 0, groups - 1)
        pulled = lax.cond(
            valid, lambda: apply_blocks(behind_coupling, couple_cols, incoming), lambda: no_couple
        )
        pulled = pulled.astype(jnp.bfloat16)
        pulled = half_planes(pulled)
        swept = forward - lax.cond(
            valid, lambda: apply_blocks(factor, cols, pulled), lambda: nothing
        )
        store = jnp.where(valid, swept, store)
        outgoing = send_out(swept.astype(jnp.bfloat16))
        return (outgoing, store)

    _, swept = lax.fori_loop(0, SEG + groups - 1, backward_step, (empty_send, empty_store))
    return swept[None]


def solution(mesh):
    return jax.shard_map(
        local,
        mesh=mesh,
        in_specs=(
            P("depth", None, "lat"),
            P("depth", "lat", None, None, None),
            P("depth", None, "lat", None, None, None),
            P("depth", "lat", None),
        ),
        out_specs=P("depth", None, "lat"),
        check_vma=False,
    )
```

profile of v0, /device:TPU:4, one launch (start us, length us, event | category | flops | bytes accessed | tf_op | source)
XLA Modules:
  0.0 528.1 jit_solution(12523199539354237369)
XLA Ops:
  4.3 268.4 %while.35 = (s32[]{:T(128)}, bf16[16,6144]{1,0:T(8,128)(2,1)S(1)}, f32[16,3072]{1,0:T(8,128)S(1)}, s32[]{:T(128)}, pred[]{:T(512)}, /*index=5*/s32[24,2]{1,0:T(8...) while((s32[]{:T(128)}, bf16[16,6144]{1,0:T(8,128)(2,1)S(1)}, ...), condition=%wide.region_5.6_spmd.clone, body=%wide.region_0.5_spmd.clone.sunk | while | flops 126175960 | bytes 15349655 | solution.py:75
  6.3 9.9 %collective-permute-done = bf16[16,6144]{1,0:T(8,128)(2,1)S(1)} collective-permute-done((bf16[16,6144]{1,0:T(8,128)(2,1)S(1)}, bf16[16,6144]{1,0:T(8,128)(2,1)S(1)}, u32[]{:S(2)}, u32[]{:S(2)}) %collective-permute-start) | collective-permute-done | bytes 196640 | tf_op jit(solution)/shard_map/while/body/eval_jaxpr/ppermute | solution.py:15
  18.9 11.1 %all_gather.42 = bf16[16,6144]{1,0:T(8,128)(2,1)S(1)} all-gather(bf16[16,3072]{1,0:T(8,128)(2,1)S(1)} %subtract_convert_fusion.3), channel_id=1, replica_groups=mesh['depth'=128,'lat'=2] {'lat'}, dimensions={1}, use_global_device_ids=true | all-gather | bytes 294912 | tf_op jit(solution)/shard_map/while/body/eval_jaxpr/all_gather | solution.py:32
  35.6 12.6 %all_gather.43 = bf16[16,6144]{1,0:T(8,128)(2,1)S(1)} all-gather(bf16[16,3072]{1,0:T(8,128)(2,1)S(1)} %get-tuple-element.767), channel_id=1, replica_groups=mesh['depth'=128,'lat'=2] {'lat'}, dimensions={1}, use_global_device_ids=true | all-gather | bytes 294912 | tf_op jit(solution)/shard_map/while/body/eval_jaxpr/all_gather | solution.py:28
  50.1 10.0 %collective-permute-done = bf16[16,6144]{1,0:T(8,128)(2,1)S(1)} collective-permute-done((bf16[16,6144]{1,0:T(8,128)(2,1)S(1)}, bf16[16,6144]{1,0:T(8,128)(2,1)S(1)}, u32[]{:S(2)}, u32[]{:S(2)}) %collective-permute-start) | collective-permute-done | bytes 196640 | tf_op jit(solution)/shard_map/while/body/eval_jaxpr/ppermute | solution.py:15
  60.1 10.1 %all_gather.42 = bf16[16,6144]{1,0:T(8,128)(2,1)S(1)} all-gather(bf16[16,3072]{1,0:T(8,128)(2,1)S(1)} %subtract_convert_fusion.3), channel_id=1, replica_groups=mesh['depth'=128,'lat'=2] {'lat'}, dimensions={1}, use_global_device_ids=true | all-gather | bytes 294912 | tf_op jit(solution)/shard_map/while/body/eval_jaxpr/all_gather | solution.py:32
  70.3 11.3 %all_gather.43 = bf16[16,6144]{1,0:T(8,128)(2,1)S(1)} all-gather(bf16[16,3072]{1,0:T(8,128)(2,1)S(1)} %get-tuple-element.767), channel_id=1, replica_groups=mesh['depth'=128,'lat'=2] {'lat'}, dimensions={1}, use_global_device_ids=true | all-gather | bytes 294912 | tf_op jit(solution)/shard_map/while/body/eval_jaxpr/all_gather | solution.py:28
  83.6 11.0 %collective-permute-done = bf16[16,6144]{1,0:T(8,128)(2,1)S(1)} collective-permute-done((bf16[16,6144]{1,0:T(8,128)(2,1)S(1)}, bf16[16,6144]{1,0:T(8,128)(2,1)S(1)}, u32[]{:S(2)}, u32[]{:S(2)}) %collective-permute-start) | collective-permute-done | bytes 196640 | tf_op jit(solution)/shard_map/while/body/eval_jaxpr/ppermute | solution.py:15
  115.3 10.8 %collective-permute-done = bf16[16,6144]{1,0:T(8,128)(2,1)S(1)} collective-permute-done((bf16[16,6144]{1,0:T(8,128)(2,1)S(1)}, bf16[16,6144]{1,0:T(8,128)(2,1)S(1)}, u32[]{:S(2)}, u32[]{:S(2)}) %collective-permute-start) | collective-permute-done | bytes 196640 | tf_op jit(solution)/shard_map/while/body/eval_jaxpr/ppermute | solution.py:15
  126.1 9.3 %all_gather.42 = bf16[16,6144]{1,0:T(8,128)(2,1)S(1)} all-gather(bf16[16,3072]{1,0:T(8,128)(2,1)S(1)} %subtract_convert_fusion.3), channel_id=1, replica_groups=mesh['depth'=128,'lat'=2] {'lat'}, dimensions={1}, use_global_device_ids=true | all-gather | bytes 294912 | tf_op jit(solution)/shard_map/while/body/eval_jaxpr/all_gather | solution.py:32
  135.5 9.5 %all_gather.43 = bf16[16,6144]{1,0:T(8,128)(2,1)S(1)} all-gather(bf16[16,3072]{1,0:T(8,128)(2,1)S(1)} %get-tuple-element.767), channel_id=1, replica_groups=mesh['depth'=128,'lat'=2] {'lat'}, dimensions={1}, use_global_device_ids=true | all-gather | bytes 294912 | tf_op jit(solution)/shard_map/while/body/eval_jaxpr/all_gather | solution.py:28
  146.9 10.4 %collective-permute-done = bf16[16,6144]{1,0:T(8,128)(2,1)S(1)} collective-permute-done((bf16[16,6144]{1,0:T(8,128)(2,1)S(1)}, bf16[16,6144]{1,0:T(8,128)(2,1)S(1)}, u32[]{:S(2)}, u32[]{:S(2)}) %collective-permute-start) | collective-permute-done | bytes 196640 | tf_op jit(solution)/shard_map/while/body/eval_jaxpr/ppermute | solution.py:15
  166.7 10.5 %all_gather.43 = bf16[16,6144]{1,0:T(8,128)(2,1)S(1)} all-gather(bf16[16,3072]{1,0:T(8,128)(2,1)S(1)} %get-tuple-element.767), channel_id=1, replica_groups=mesh['depth'=128,'lat'=2] {'lat'}, dimensions={1}, use_global_device_ids=true | all-gather | bytes 294912 | tf_op jit(solution)/shard_map/while/body/eval_jaxpr/all_gather | solution.py:28
  179.1 9.9 %collective-permute-done = bf16[16,6144]{1,0:T(8,128)(2,1)S(1)} collective-permute-done((bf16[16,6144]{1,0:T(8,128)(2,1)S(1)}, bf16[16,6144]{1,0:T(8,128)(2,1)S(1)}, u32[]{:S(2)}, u32[]{:S(2)}) %collective-permute-start) | collective-permute-done | bytes 196640 | tf_op jit(solution)/shard_map/while/body/eval_jaxpr/ppermute | solution.py:15
  189.0 9.3 %all_gather.42 = bf16[16,6144]{1,0:T(8,128)(2,1)S(1)} all-gather(bf16[16,3072]{1,0:T(8,128)(2,1)S(1)} %subtract_convert_fusion.3), channel_id=1, replica_groups=mesh['depth'=128,'lat'=2] {'lat'}, dimensions={1}, use_global_device_ids=true | all-gather | bytes 294912 | tf_op jit(solution)/shard_map/while/body/eval_jaxpr/all_gather | solution.py:32
  198.4 9.8 %all_gather.43 = bf16[16,6144]{1,0:T(8,128)(2,1)S(1)} all-gather(bf16[16,3072]{1,0:T(8,128)(2,1)S(1)} %get-tuple-element.767), channel_id=1, replica_groups=mesh['depth'=128,'lat'=2] {'lat'}, dimensions={1}, use_global_device_ids=true | all-gather | bytes 294912 | tf_op jit(solution)/shard_map/while/body/eval_jaxpr/all_gather | solution.py:28
  210.2 11.8 %collective-permute-done = bf16[16,6144]{1,0:T(8,128)(2,1)S(1)} collective-permute-done((bf16[16,6144]{1,0:T(8,128)(2,1)S(1)}, bf16[16,6144]{1,0:T(8,128)(2,1)S(1)}, u32[]{:S(2)}, u32[]{:S(2)}) %collective-permute-start) | collective-permute-done | bytes 196640 | tf_op jit(solution)/shard_map/while/body/eval_jaxpr/ppermute | solution.py:15
  242.5 9.9 %collective-permute-done = bf16[16,6144]{1,0:T(8,128)(2,1)S(1)} collective-permute-done((bf16[16,6144]{1,0:T(8,128)(2,1)S(1)}, bf16[16,6144]{1,0:T(8,128)(2,1)S(1)}, u32[]{:S(2)}, u32[]{:S(2)}) %collective-permute-start) | collective-permute-done | bytes 196640 | tf_op jit(solution)/shard_map/while/body/eval_jaxpr/ppermute | solution.py:15
  252.4 9.9 %all_gather.42 = bf16[16,6144]{1,0:T(8,128)(2,1)S(1)} all-gather(bf16[16,3072]{1,0:T(8,128)(2,1)S(1)} %subtract_convert_fusion.3), channel_id=1, replica_groups=mesh['depth'=128,'lat'=2] {'lat'}, dimensions={1}, use_global_device_ids=true | all-gather | bytes 294912 | tf_op jit(solution)/shard_map/while/body/eval_jaxpr/all_gather | solution.py:32
  262.4 10.3 %all_gather.43 = bf16[16,6144]{1,0:T(8,128)(2,1)S(1)} all-gather(bf16[16,3072]{1,0:T(8,128)(2,1)S(1)} %get-tuple-element.767), channel_id=1, replica_groups=mesh['depth'=128,'lat'=2] {'lat'}, dimensions={1}, use_global_device_ids=true | all-gather | bytes 294912 | tf_op jit(solution)/shard_map/while/body/eval_jaxpr/all_gather | solution.py:28
  272.7 254.8 %while.36 = (s32[]{:T(128)}, bf16[16,6144]{1,0:T(8,128)(2,1)S(1)}, f32[16,3072]{1,0:T(8,128)S(1)}, s32[]{:T(128)}, pred[]{:T(512)}, /*index=5*/s32[24,2]{1,0:T(8...) while((s32[]{:T(128)}, bf16[16,6144]{1,0:T(8,128)(2,1)S(1)}, ...), condition=%wide.region_11.12_spmd.clone, body=%wide.region_6.11_spmd.clone.sunk | while | flops 126126808 | bytes 14759831 | solution.py:96
  283.2 9.8 %all_gather.44 = bf16[16,6144]{1,0:T(8,128)(2,1)S(1)} all-gather(bf16[16,3072]{1,0:T(8,128)(2,1)S(1)} %get-tuple-element.855), channel_id=1, replica_groups=mesh['depth'=128,'lat'=2] {'lat'}, dimensions={1}, use_global_device_ids=true | all-gather | bytes 294912 | tf_op jit(solution)/shard_map/while/body/eval_jaxpr/all_gather | solution.py:32
  293.1 9.9 %all_gather.45 = bf16[16,6144]{1,0:T(8,128)(2,1)S(1)} all-gather(bf16[16,3072]{1,0:T(8,128)(2,1)S(1)} %get-tuple-element.779), channel_id=1, replica_groups=mesh['depth'=128,'lat'=2] {'lat'}, dimensions={1}, use_global_device_ids=true | all-gather | bytes 294912 | tf_op jit(solution)/shard_map/while/body/eval_jaxpr/all_gather | solution.py:28
  303.0 11.9 %collective-permute-start.1 = (bf16[16,6144]{1,0:T(8,128)(2,1)S(1)}, bf16[16,6144]{1,0:T(8,128)(2,1)S(1)}, u32[]{:S(2)}, u32[]{:S(2)}) collective-permute-start(bf16[16,6144]{1,0:T(8,128)(2,1)S(1)} %get-tuple-element.830), channel_id=1, source_target_pairs={{2,0},{4,2},{6,4},{8,6},{10,8},{12,10},{14,12},{16,14},{18,16},{20... | collective-permute-start | bytes 589832 | tf_op jit(solution)/shard_map/while/body/eval_jaxpr/ppermute | solution.py:15
  318.1 10.2 %all_gather.44 = bf16[16,6144]{1,0:T(8,128)(2,1)S(1)} all-gather(bf16[16,3072]{1,0:T(8,128)(2,1)S(1)} %get-tuple-element.855), channel_id=1, replica_groups=mesh['depth'=128,'lat'=2] {'lat'}, dimensions={1}, use_global_device_ids=true | all-gather | bytes 294912 | tf_op jit(solution)/shard_map/while/body/eval_jaxpr/all_gather | solution.py:32
  328.4 9.4 %all_gather.45 = bf16[16,6144]{1,0:T(8,128)(2,1)S(1)} all-gather(bf16[16,3072]{1,0:T(8,128)(2,1)S(1)} %get-tuple-element.779), channel_id=1, replica_groups=mesh['depth'=128,'lat'=2] {'lat'}, dimensions={1}, use_global_device_ids=true | all-gather | bytes 294912 | tf_op jit(solution)/shard_map/while/body/eval_jaxpr/all_gather | solution.py:28
  348.6 11.2 %all_gather.44 = bf16[16,6144]{1,0:T(8,128)(2,1)S(1)} all-gather(bf16[16,3072]{1,0:T(8,128)(2,1)S(1)} %get-tuple-element.855), channel_id=1, replica_groups=mesh['depth'=128,'lat'=2] {'lat'}, dimensions={1}, use_global_device_ids=true | all-gather | bytes 294912 | tf_op jit(solution)/shard_map/while/body/eval_jaxpr/all_gather | solution.py:32
  360.0 9.3 %all_gather.45 = bf16[16,6144]{1,0:T(8,128)(2,1)S(1)} all-gather(bf16[16,3072]{1,0:T(8,128)(2,1)S(1)} %get-tuple-element.779), channel_id=1, replica_groups=mesh['depth'=128,'lat'=2] {'lat'}, dimensions={1}, use_global_device_ids=true | all-gather | bytes 294912 | tf_op jit(solution)/shard_map/while/body/eval_jaxpr/all_gather | solution.py:28
  410.2 9.4 %all_gather.44 = bf16[16,6144]{1,0:T(8,128)(2,1)S(1)} all-gather(bf16[16,3072]{1,0:T(8,128)(2,1)S(1)} %get-tuple-element.855), channel_id=1, replica_groups=mesh['depth'=128,'lat'=2] {'lat'}, dimensions={1}, use_global_device_ids=true | all-gather | bytes 294912 | tf_op jit(solution)/shard_map/while/body/eval_jaxpr/all_gather | solution.py:32
  441.7 9.5 %all_gather.44 = bf16[16,6144]{1,0:T(8,128)(2,1)S(1)} all-gather(bf16[16,3072]{1,0:T(8,128)(2,1)S(1)} %get-tuple-element.855), channel_id=1, replica_groups=mesh['depth'=128,'lat'=2] {'lat'}, dimensions={1}, use_global_device_ids=true | all-gather | bytes 294912 | tf_op jit(solution)/shard_map/while/body/eval_jaxpr/all_gather | solution.py:32
  451.4 9.3 %all_gather.45 = bf16[16,6144]{1,0:T(8,128)(2,1)S(1)} all-gather(bf16[16,3072]{1,0:T(8,128)(2,1)S(1)} %get-tuple-element.779), channel_id=1, replica_groups=mesh['depth'=128,'lat'=2] {'lat'}, dimensions={1}, use_global_device_ids=true | all-gather | bytes 294912 | tf_op jit(solution)/shard_map/while/body/eval_jaxpr/all_gather | solution.py:28
  481.2 9.4 %all_gather.45 = bf16[16,6144]{1,0:T(8,128)(2,1)S(1)} all-gather(bf16[16,3072]{1,0:T(8,128)(2,1)S(1)} %get-tuple-element.779), channel_id=1, replica_groups=mesh['depth'=128,'lat'=2] {'lat'}, dimensions={1}, use_global_device_ids=true | all-gather | bytes 294912 | tf_op jit(solution)/shard_map/while/body/eval_jaxpr/all_gather | solution.py:28
  (156 shorter events, 236.1 us)
Async XLA Ops:
  0.8 3.5 copy-start
  4.3 11.8 %collective-permute-start = (bf16[16,6144]{1,0:T(8,128)(2,1)S(1)}, bf16[16,6144]{1,0:T(8,128)(2,1)S(1)}, u32[]{:S(2)}, u32[]{:S(2)}) collective-permute-start(bf16[16,6144]{1,0:T(8,128)(2,1)S(1)} %get-tuple-element.794), channel_id=1, source_target_pairs={{0,2},{2,4},{4,6},{6,8},{8,10},{10,12},{12,14},{14,16},{16,18},{18... | collective-permute-start | bytes 589832 | tf_op jit(solution)/shard_map/while/body/eval_jaxpr/ppermute | solution.py:15
  48.2 11.9 %collective-permute-start = (bf16[16,6144]{1,0:T(8,128)(2,1)S(1)}, bf16[16,6144]{1,0:T(8,128)(2,1)S(1)}, u32[]{:S(2)}, u32[]{:S(2)}) collective-permute-start(bf16[16,6144]{1,0:T(8,128)(2,1)S(1)} %get-tuple-element.794), channel_id=1, source_target_pairs={{0,2},{2,4},{4,6},{6,8},{8,10},{10,12},{12,14},{14,16},{16,18},{18... | collective-permute-start | bytes 589832 | tf_op jit(solution)/shard_map/while/body/eval_jaxpr/ppermute | solution.py:15
  81.6 12.9 %collective-permute-start = (bf16[16,6144]{1,0:T(8,128)(2,1)S(1)}, bf16[16,6144]{1,0:T(8,128)(2,1)S(1)}, u32[]{:S(2)}, u32[]{:S(2)}) collective-permute-start(bf16[16,6144]{1,0:T(8,128)(2,1)S(1)} %get-tuple-element.794), channel_id=1, source_target_pairs={{0,2},{2,4},{4,6},{6,8},{8,10},{10,12},{12,14},{14,16},{16,18},{18... | collective-permute-start | bytes 589832 | tf_op jit(solution)/shard_map/while/body/eval_jaxpr/ppermute | solution.py:15
  113.3 12.7 %collective-permute-start = (bf16[16,6144]{1,0:T(8,128)(2,1)S(1)}, bf16[16,6144]{1,0:T(8,128)(2,1)S(1)}, u32[]{:S(2)}, u32[]{:S(2)}) collective-permute-start(bf16[16,6144]{1,0:T(8,128)(2,1)S(1)} %get-tuple-element.794), channel_id=1, source_target_pairs={{0,2},{2,4},{4,6},{6,8},{8,10},{10,12},{12,14},{14,16},{16,18},{18... | collective-permute-start | bytes 589832 | tf_op jit(solution)/shard_map/while/body/eval_jaxpr/ppermute | solution.py:15
  145.0 12.4 %collective-permute-start = (bf16[16,6144]{1,0:T(8,128)(2,1)S(1)}, bf16[16,6144]{1,0:T(8,128)(2,1)S(1)}, u32[]{:S(2)}, u32[]{:S(2)}) collective-permute-start(bf16[16,6144]{1,0:T(8,128)(2,1)S(1)} %get-tuple-element.794), channel_id=1, source_target_pairs={{0,2},{2,4},{4,6},{6,8},{8,10},{10,12},{12,14},{14,16},{16,18},{18... | collective-permute-start | bytes 589832 | tf_op jit(solution)/shard_map/while/body/eval_jaxpr/ppermute | solution.py:15
  177.2 11.8 %collective-permute-start = (bf16[16,6144]{1,0:T(8,128)(2,1)S(1)}, bf16[16,6144]{1,0:T(8,128)(2,1)S(1)}, u32[]{:S(2)}, u32[]{:S(2)}) collective-permute-start(bf16[16,6144]{1,0:T(8,128)(2,1)S(1)} %get-tuple-element.794), channel_id=1, source_target_pairs={{0,2},{2,4},{4,6},{6,8},{8,10},{10,12},{12,14},{14,16},{16,18},{18... | collective-permute-start | bytes 589832 | tf_op jit(solution)/shard_map/while/body/eval_jaxpr/ppermute | solution.py:15
  208.2 13.8 %collective-permute-start = (bf16[16,6144]{1,0:T(8,128)(2,1)S(1)}, bf16[16,6144]{1,0:T(8,128)(2,1)S(1)}, u32[]{:S(2)}, u32[]{:S(2)}) collective-permute-start(bf16[16,6144]{1,0:T(8,128)(2,1)S(1)} %get-tuple-element.794), channel_id=1, source_target_pairs={{0,2},{2,4},{4,6},{6,8},{8,10},{10,12},{12,14},{14,16},{16,18},{18... | collective-permute-start | bytes 589832 | tf_op jit(solution)/shard_map/while/body/eval_jaxpr/ppermute | solution.py:15
  240.6 11.8 %collective-permute-start = (bf16[16,6144]{1,0:T(8,128)(2,1)S(1)}, bf16[16,6144]{1,0:T(8,128)(2,1)S(1)}, u32[]{:S(2)}, u32[]{:S(2)}) collective-permute-start(bf16[16,6144]{1,0:T(8,128)(2,1)S(1)} %get-tuple-element.794), channel_id=1, source_target_pairs={{0,2},{2,4},{4,6},{6,8},{8,10},{10,12},{12,14},{14,16},{16,18},{18... | collective-permute-start | bytes 589832 | tf_op jit(solution)/shard_map/while/body/eval_jaxpr/ppermute | solution.py:15
  272.7 10.4 %collective-permute-start.1 = (bf16[16,6144]{1,0:T(8,128)(2,1)S(1)}, bf16[16,6144]{1,0:T(8,128)(2,1)S(1)}, u32[]{:S(2)}, u32[]{:S(2)}) collective-permute-start(bf16[16,6144]{1,0:T(8,128)(2,1)S(1)} %get-tuple-element.830), channel_id=1, source_target_pairs={{2,0},{4,2},{6,4},{8,6},{10,8},{12,10},{14,12},{16,14},{18,16},{20... | collective-permute-start | bytes 589832 | tf_op jit(solution)/shard_map/while/body/eval_jaxpr/ppermute | solution.py:15
  303.0 15.1 %collective-permute-start.1 = (bf16[16,6144]{1,0:T(8,128)(2,1)S(1)}, bf16[16,6144]{1,0:T(8,128)(2,1)S(1)}, u32[]{:S(2)}, u32[]{:S(2)}) collective-permute-start(bf16[16,6144]{1,0:T(8,128)(2,1)S(1)} %get-tuple-element.830), channel_id=1, source_target_pairs={{2,0},{4,2},{6,4},{8,6},{10,8},{12,10},{14,12},{16,14},{18,16},{20... | collective-permute-start | bytes 589832 | tf_op jit(solution)/shard_map/while/body/eval_jaxpr/ppermute | solution.py:15
  337.8 10.8 %collective-permute-start.1 = (bf16[16,6144]{1,0:T(8,128)(2,1)S(1)}, bf16[16,6144]{1,0:T(8,128)(2,1)S(1)}, u32[]{:S(2)}, u32[]{:S(2)}) collective-permute-start(bf16[16,6144]{1,0:T(8,128)(2,1)S(1)} %get-tuple-element.830), channel_id=1, source_target_pairs={{2,0},{4,2},{6,4},{8,6},{10,8},{12,10},{14,12},{16,14},{18,16},{20... | collective-permute-start | bytes 589832 | tf_op jit(solution)/shard_map/while/body/eval_jaxpr/ppermute | solution.py:15
  369.3 9.6 %collective-permute-start.1 = (bf16[16,6144]{1,0:T(8,128)(2,1)S(1)}, bf16[16,6144]{1,0:T(8,128)(2,1)S(1)}, u32[]{:S(2)}, u32[]{:S(2)}) collective-permute-start(bf16[16,6144]{1,0:T(8,128)(2,1)S(1)} %get-tuple-element.830), channel_id=1, source_target_pairs={{2,0},{4,2},{6,4},{8,6},{10,8},{12,10},{14,12},{16,14},{18,16},{20... | collective-permute-start | bytes 589832 | tf_op jit(solution)/shard_map/while/body/eval_jaxpr/ppermute | solution.py:15
  397.5 12.7 %collective-permute-start.1 = (bf16[16,6144]{1,0:T(8,128)(2,1)S(1)}, bf16[16,6144]{1,0:T(8,128)(2,1)S(1)}, u32[]{:S(2)}, u32[]{:S(2)}) collective-permute-start(bf16[16,6144]{1,0:T(8,128)(2,1)S(1)} %get-tuple-element.830), channel_id=1, source_target_pairs={{2,0},{4,2},{6,4},{8,6},{10,8},{12,10},{14,12},{16,14},{18,16},{20... | collective-permute-start | bytes 589832 | tf_op jit(solution)/shard_map/while/body/eval_jaxpr/ppermute | solution.py:15
  429.0 12.7 %collective-permute-start.1 = (bf16[16,6144]{1,0:T(8,128)(2,1)S(1)}, bf16[16,6144]{1,0:T(8,128)(2,1)S(1)}, u32[]{:S(2)}, u32[]{:S(2)}) collective-permute-start(bf16[16,6144]{1,0:T(8,128)(2,1)S(1)} %get-tuple-element.830), channel_id=1, source_target_pairs={{2,0},{4,2},{6,4},{8,6},{10,8},{12,10},{14,12},{16,14},{18,16},{20... | collective-permute-start | bytes 589832 | tf_op jit(solution)/shard_map/while/body/eval_jaxpr/ppermute | solution.py:15
  460.7 11.1 %collective-permute-start.1 = (bf16[16,6144]{1,0:T(8,128)(2,1)S(1)}, bf16[16,6144]{1,0:T(8,128)(2,1)S(1)}, u32[]{:S(2)}, u32[]{:S(2)}) collective-permute-start(bf16[16,6144]{1,0:T(8,128)(2,1)S(1)} %get-tuple-element.830), channel_id=1, source_target_pairs={{2,0},{4,2},{6,4},{8,6},{10,8},{12,10},{14,12},{16,14},{18,16},{20... | collective-permute-start | bytes 589832 | tf_op jit(solution)/shard_map/while/body/eval_jaxpr/ppermute | solution.py:15
  490.5 11.6 %collective-permute-start.1 = (bf16[16,6144]{1,0:T(8,128)(2,1)S(1)}, bf16[16,6144]{1,0:T(8,128)(2,1)S(1)}, u32[]{:S(2)}, u32[]{:S(2)}) collective-permute-start(bf16[16,6144]{1,0:T(8,128)(2,1)S(1)} %get-tuple-element.830), channel_id=1, source_target_pairs={{2,0},{4,2},{6,4},{8,6},{10,8},{12,10},{14,12},{16,14},{18,16},{20... | collective-permute-start | bytes 589832 | tf_op jit(solution)/shard_map/while/body/eval_jaxpr/ppermute | solution.py:15
  527.4 0.7 copy-start.1
where the time goes:
time: 529 us; the launch traced here: 528 us
  blocking collectives  313 us (59%)
  waiting for transfers between devices  117 us (22%)
  starting transfers between devices  75.4 us (14%)
  matrix products  11.5 us (2%)
  local copies, waits for them, and re-layouts  8.66 us (2%)
    all_gather x16, blocking collectives, planes(): return lax.all_gather(vector, 'lat', axis=1, tiled=True)  157 us
    all_gather x16, blocking collectives, half_planes(): return lax.all_gather(vector, 'lat', axis=1, tiled=True)  155 us
    ppermute x16, waiting for transfers between devices, shifted(): return lax.ppermute(block, axis, route)  117 us
    ppermute x16, starting transfers between devices, shifted(): return lax.ppermute(block, axis, route)  75.4 us
    dot_general x4, matrix products, apply_blocks(): jnp.einsum('rkij,srkj->sri', blocks, picked, preferred_element_type=jnp.f...  11.5 us
  transfers between devices with their start and end apart: 16, of which 16 were waited for; matrix products, arithmetic and copies ran while one was open for 0% of the time, Pallas kernels for 0%

commit v1 on v0

v1 whole, which is shorter than its diff:
```python
import functools

import jax
import jax.numpy as jnp
from jax import lax
from jax.experimental import pallas as pl
from jax.experimental.pallas import tpu as pltpu
from jax.sharding import PartitionSpec as P

MESH = pl.DeviceIdType.MESH
BLK = 128
KH = 8
KC = 2
SEG = 8
SHOTS = 16
NBR = 48
HALF = 24
CHUNKS = 4
ROWS = HALF // CHUNKS
F32 = jnp.float32
BF16 = jnp.bfloat16
NN = (((1,), (0,)), ((), ()))
NT = (((1,), (1,)), ((), ()))


def gathered(vector, cols, row, count):
    return jnp.concatenate([vector[cols[row, k]] for k in range(count)], axis=1)


def row_apply(blocks, vector, cols, row, count):
    operand = gathered(vector, cols, row, count)
    weights = blocks[row].reshape(count * BLK, BLK)
    return lax.dot_general(operand, weights, NN, preferred_element_type=F32)


def row_apply_plain(blocks, vector, cols, row, count):
    operand = gathered(vector, cols, row, count)
    weights = jnp.concatenate([blocks[row, k] for k in range(count)], axis=1)
    return lax.dot_general(operand, weights, NT, preferred_element_type=F32)


def transpose_blocks(blocks, rows, count):
    def one(row, carry):
        for k in range(count):
            blocks[row, k] = blocks[row, k].T
        return carry

    lax.fori_loop(0, rows, one, 0, unroll=2)


def sweep_kernel(
    sources, frontal, couplings, cols, swept,
    factor, ahead, behind, field, incoming, later, reduced, pulled, out_fwd, out_bwd,
    load_sem, lat_send, lat_recv, fwd_send, fwd_recv, bwd_send, bwd_recv,
):
    depth = lax.axis_index("depth")
    half = lax.axis_index("lat")
    place = lax.rem(depth, SEG)
    other = 1 - half
    base = half * HALF

    load_factor = pltpu.make_async_copy(frontal, factor, load_sem.at[0])
    load_ahead = pltpu.make_async_copy(couplings.at[0], ahead, load_sem.at[1])
    load_behind = pltpu.make_async_copy(couplings.at[1], behind, load_sem.at[2])
    load_factor.start()
    load_ahead.start()
    load_behind.start()

    barrier = pltpu.get_barrier_semaphore()
    pl.semaphore_signal(barrier, inc=1, device_id=(depth, other), device_id_type=MESH)

    @pl.when(place > 0)
    def _():
        for lat in range(2):
            pl.semaphore_signal(barrier, inc=1, device_id=(depth - 1, lat), device_id_type=MESH)

    @pl.when(place < SEG - 1)
    def _():
        for lat in range(2):
            pl.semaphore_signal(barrier, inc=1, device_id=(depth + 1, lat), device_id_type=MESH)

    at_edge = jnp.logical_or(place == 0, place == SEG - 1)
    pl.semaphore_wait(barrier, jnp.where(at_edge, 3, 5))

    def across(vector, slot):
        mine = vector.at[pl.ds(base, HALF)]
        return pltpu.make_async_remote_copy(
            src_ref=mine, dst_ref=mine, send_sem=lat_send.at[slot], recv_sem=lat_recv.at[slot],
            device_id=(depth, other), device_id_type=MESH,
        )

    def arriving_across(vector, slot):
        theirs = vector.at[pl.ds(other * HALF, HALF)]
        return pltpu.make_async_remote_copy(
            src_ref=theirs, dst_ref=theirs, send_sem=lat_send.at[slot], recv_sem=lat_recv.at[slot],
            device_id=(depth, other), device_id_type=MESH,
        )

    def chunk_copy(source, target, chunk, far, owner, step, send, recv):
        lat = other if far else half
        return pltpu.make_async_remote_copy(
            src_ref=source.at[pl.ds(chunk * ROWS, ROWS)],
            dst_ref=target.at[pl.ds(owner * HALF + chunk * ROWS, ROWS)],
            send_sem=send.at[far, chunk], recv_sem=recv.at[far, chunk],
            device_id=(depth + step, lat), device_id_type=MESH,
        )

    def forward_copy(chunk, far, owner):
        return chunk_copy(out_fwd, incoming, chunk, far, owner, 1, fwd_send, fwd_recv)

    def backward_copy(chunk, far, owner):
        return chunk_copy(out_bwd, later, chunk, far, owner, -1, bwd_send, bwd_recv)

    def wait_arrivals(make):
        for far in range(2):
            owner = other if far else half
            for chunk in range(CHUNKS):
                make(chunk, far, owner).wait_recv()

    def start_chunk(make, chunk):
        for far in (1, 0):
            make(chunk, far, half).start()

    def wait_sent(make):
        for far in range(2):
            for chunk in range(CHUNKS):
                make(chunk, far, half).wait_send()

    @pl.when(place == 0)
    def _():
        for row in range(HALF):
            reduced[base + row] = sources[:, row * BLK:(row + 1) * BLK].astype(BF16)

    @pl.when(place > 0)
    def _():
        load_ahead.wait()
        transpose_blocks(ahead, HALF, KC)
        load_factor.wait()
        transpose_blocks(factor, HALF, KH)
        wait_arrivals(forward_copy)
        for row in range(HALF):
            coupled = row_apply(ahead, incoming, cols, row, KC)
            reduced[base + row] = (sources[:, row * BLK:(row + 1) * BLK] - coupled).astype(BF16)

    send_reduced = across(reduced, 0)
    send_reduced.start()
    arriving_across(reduced, 0).wait_recv()

    @pl.when(place == 0)
    def _():
        load_ahead.wait()
        load_factor.wait()
        for chunk in range(CHUNKS):
            for row in range(chunk * ROWS, (chunk + 1) * ROWS):
                value = row_apply_plain(factor, reduced, cols, row, KH)
                field[row] = value
                out_fwd[row] = value.astype(BF16)
            start_chunk(forward_copy, chunk)
        transpose_blocks(factor, HALF, KH)

    @pl.when(place > 0)
    def _():
        for chunk in range(CHUNKS):
            for row in range(chunk * ROWS, (chunk + 1) * ROWS):
                value = row_apply(factor, reduced, cols, row, KH)
                field[row] = value
                out_fwd[row] = value.astype(BF16)

            @pl.when(place < SEG - 1)
            def _():
                start_chunk(forward_copy, chunk)

            @pl.when(place == SEG - 1)
            def _():
                for row in range(chunk * ROWS, (chunk + 1) * ROWS):
                    out_bwd[row] = out_fwd[row]
                start_chunk(backward_copy, chunk)

    load_behind.wait()

    @pl.when(place == SEG - 1)
    def _():
        for row in range(HALF):
            swept[:, row * BLK:(row + 1) * BLK] = field[row]

    @pl.when(place < SEG - 1)
    def _():
        transpose_blocks(behind, HALF, KC)
        wait_arrivals(backward_copy)
        for row in range(HALF):
            pulled[base + row] = row_apply(behind, later, cols, row, KC).astype(BF16)
        send_pulled = across(pulled, 1)
        send_pulled.start()
        arriving_across(pulled, 1).wait_recv()
        for chunk in range(CHUNKS):
            for row in range(chunk * ROWS, (chunk + 1) * ROWS):
                value = field[row] - row_apply(factor, pulled, cols, row, KH)
                swept[:, row * BLK:(row + 1) * BLK] = value
                out_bwd[row] = value.astype(BF16)

            @pl.when(place > 0)
            def _():
                start_chunk(backward_copy, chunk)

        send_pulled.wait_send()
        wait_sent(forward_copy)

    @pl.when(place > 0)
    def _():
        wait_sent(backward_copy)

    send_reduced.wait_send()


def local(sources, frontal, couplings, pattern):
    vector = pltpu.VMEM((NBR, SHOTS, BLK), BF16)
    half_vector = pltpu.VMEM((HALF, SHOTS, BLK), BF16)
    vmem = pl.BlockSpec(memory_space=pltpu.VMEM)
    hbm = pl.BlockSpec(memory_space=pl.ANY)
    smem = pl.BlockSpec(memory_space=pltpu.SMEM)
    out = pl.pallas_call(
        sweep_kernel,
        out_shape=jax.ShapeDtypeStruct((SHOTS, HALF * BLK), F32),
        in_specs=[vmem, hbm, hbm, smem],
        out_specs=vmem,
        scratch_shapes=[
            pltpu.VMEM((HALF, KH, BLK, BLK), BF16),
            pltpu.VMEM((HALF, KC, BLK, BLK), BF16),
            pltpu.VMEM((HALF, KC, BLK, BLK), BF16),
            pltpu.VMEM((HALF, SHOTS, BLK), F32),
            vector, vector, vector, vector, half_vector, half_vector,
            pltpu.SemaphoreType.DMA((3,)),
            pltpu.SemaphoreType.DMA((2,)),
            pltpu.SemaphoreType.DMA((2,)),
            pltpu.SemaphoreType.DMA((2, CHUNKS)),
            pltpu.SemaphoreType.DMA((2, CHUNKS)),
            pltpu.SemaphoreType.DMA((2, CHUNKS)),
            pltpu.SemaphoreType.DMA((2, CHUNKS)),
        ],
        compiler_params=pltpu.CompilerParams(
            collective_id=0, has_side_effects=True, vmem_limit_bytes=48 * 1024 * 1024
        ),
    )(sources[0], frontal[0], couplings[0], pattern[0])
    return out[None]


def solution(mesh):
    return jax.shard_map(
        local,
        mesh=mesh,
        in_specs=(
            P("depth", None, "lat"),
            P("depth", "lat", None, None, None),
            P("depth", None, "lat", None, None, None),
            P("depth", "lat", None),
        ),
        out_specs=P("depth", None, "lat"),
        check_vma=False,
    )
```

time: 529 us -> 172 us (0.33)
  blocking collectives: 313 us -> 0 us
  Pallas kernels: 0 us -> 168 us
  waiting for transfers between devices: 117 us -> 0 us
  starting transfers between devices: 75.4 us -> 0 us
  matrix products: 11.5 us -> 0 us
    all_gather x32 -> x0, blocking collectives: 313 us -> none  [the longest x16 157 us: planes(): return lax.all_gather(vector, 'lat', axis=1, tiled=True)]
    pallas_call x0 -> x1, Pallas kernels: none -> 168 us  [local(): pl.pallas_call(sweep_kernel, out_shape=jax.ShapeDtypeStruct((SHOTS, HALF...]
    ppermute x16 -> x0, waiting for transfers between devices: 117 us -> none  [shifted(): return lax.ppermute(block, axis, route)]
    ppermute x16 -> x0, starting transfers between devices: 75.4 us -> none  [shifted(): return lax.ppermute(block, axis, route)]
    dot_general x4 -> x0, matrix products: 11.5 us -> none  [apply_blocks(): jnp.einsum('rkij,srkj->sri', blocks, picked, preferred_element_type=jnp.f...]
  transfers between devices with their start and end apart: 16 -> 0, of which waited for: 16 -> 0; matrix products, arithmetic and copies ran while one was open for 0% -> 0% of each run, Pallas kernels for 0% -> 0%
where the time goes in v1:
time: 172 us
  Pallas kernels  168 us (98%)
  local copies, waits for them, and re-layouts  4.25 us (2%)
    pallas_call x1, Pallas kernels, local(): pl.pallas_call(sweep_kernel, out_shape=jax.ShapeDtypeStruct((SHOTS, HALF...  168 us
    unnamed x6, local copies, waits for them, and re-layouts  4.25 us

profile of v1, /device:TPU:4, one launch (start us, length us, event | category | flops | bytes accessed | tf_op | source)
XLA Modules:
  0.0 172.3 jit_solution(2745065029966369614)
XLA Ops:
  0.0 0.8 copy.5
  0.8 0.0 copy-start
  0.8 1.9 %copy-done = bf16[1,2,24,2,128,128]{5,4,3,2,1,0:T(8,128)(2,1)S(1)} copy-done((bf16[1,2,24,2,128,128]{5,4,3,2,1,0:T(8,128)(2,1)S(1)}, bf16[1,2,24,2,128,128]{5,4,3,2,1,0:T(8,128)(2,1)}, u32[]{:S(2)}) %copy-start) | copy-done | bytes 3145752
  2.6 0.0 copy-start.1
  2.7 0.9 copy-done.1
  3.6 168.0 %shard_map.46 = f32[16,3072]{1,0:T(8,128)S(1)} custom-call(f32[16,3072]{1,0:T(8,128)S(1)} %bitcast.7, bf16[24,8,128,128]{3,2,1,0:T(8,128)(2,1)} %bitcast.9, bf16[2,24,2,128,128]{4,3,2,1,0:T(8,128)(2,1)S(1)} %bitcast.5, s32[24,8]{1,0:T(8,128)S(1)} %bitcast.8), custom_call_target="tpu_custom_call" | custom-call | tf_op jit(solution)/shard_map/pallas_call | solution.py:221
  171.6 0.7 copy.7
Async XLA Ops:
  0.8 1.9 %copy-start = (bf16[1,2,24,2,128,128]{5,4,3,2,1,0:T(8,128)(2,1)S(1)}, bf16[1,2,24,2,128,128]{5,4,3,2,1,0:T(8,128)(2,1)}, u32[]{:S(2)}) copy-start(bf16[1,2,24,2,128,128]{5,4,3,2,1,0:T(8,128)(2,1)} %param.6) | copy-start | bytes 9437188
  2.6 0.9 copy-start.1

commit v2 on v1

v2 whole, which is shorter than its diff:
```python
import jax
import jax.numpy as jnp
from jax import lax
from jax.experimental import pallas as pl
from jax.experimental.pallas import tpu as pltpu
from jax.sharding import PartitionSpec as P

MESH = pl.DeviceIdType.MESH
BLK = 128
KH = 8
KC = 2
SEG = 8
SHOTS = 16
NBR = 48
HALF = 24
CHUNKS = 4
ROWS = HALF // CHUNKS
F32 = jnp.float32
BF16 = jnp.bfloat16
NN = (((1,), (0,)), ((), ()))

SWAP_AHEAD = (2,)
SWAP_BEHIND = ()
AHEAD, BEHIND = range(2)
AFTER_START = ()
AT_FORWARD = ((0, 4, AHEAD), (1, 5, AHEAD), (1, 6, AHEAD), (2, 7, AHEAD), (6, 1, BEHIND))
AT_BACKWARD = ((6, 2, BEHIND),)
PACE_AHEAD = (0, 24, 0, 24, 2, 2, 2, 2)
PACE_BEHIND = (12, 3, 4, 12, 3, 4, 24, 0)
FIRST_AHEAD = (1, 3)
FIRST_BEHIND = (6,)
PACES = (PACE_AHEAD, PACE_BEHIND)
AFTER_START = tuple(told for told in AFTER_START if PACES[told[2]][told[1]])
AT_FORWARD = tuple(told for told in AT_FORWARD if PACES[told[2]][told[1]])
AT_BACKWARD = tuple(told for told in AT_BACKWARD if PACES[told[2]][told[1]])
TOLD = AFTER_START + AT_FORWARD + AT_BACKWARD
GREETS = tuple(sorted({(min(i, j), max(i, j)) for i, j, _ in TOLD if abs(i - j) > 1}))


def any_of(place, places):
    found = place < 0
    for one in places:
        found = jnp.logical_or(found, place == one)
    return found


def dot(operand, weights):
    return lax.dot_general(operand, weights, NN, preferred_element_type=F32)


def gathered(vector, cols, row, count):
    return jnp.concatenate([vector[cols[k, row]] for k in range(count)], axis=1)


def row_apply(blocks, vector, cols, row):
    return dot(gathered(vector, cols, row, KH), blocks[row].reshape(KH * BLK, BLK))


def transpose_factor(blocks):
    def one(row, carry):
        for k in range(KH):
            blocks[row, k] = blocks[row, k].T
        return carry

    lax.fori_loop(0, HALF, one, 0, unroll=2)


def split_couplings(raw, diagonal, beside, base):
    def one(row, carry):
        diagonal[row] = raw[row, 0].T
        beside[base + row] = raw[row, 1].T
        return carry

    lax.fori_loop(0, HALF, one, 0, unroll=4)


def sweep_kernel(
    sources_hbm, frontal, couplings, pattern, cols, swept,
    sources, partial, factor, raw, diag_ahead, diag_behind, side_ahead, side_behind, diag_next, diag_prior,
    rounded, source_next, their_pattern, their_cols, field, incoming, later, incoming_plus, later_plus, reduced, pulled, out_fwd, out_bwd,
    load_sem, once_send, once_recv, fwd_send, fwd_recv, bwd_send, bwd_recv, go,
):
    depth = lax.axis_index("depth")
    half = lax.axis_index("lat")
    place = lax.rem(depth, SEG)
    other = 1 - half
    base = half * HALF
    their_base = other * HALF

    load_factor = pltpu.make_async_copy(frontal, factor, load_sem.at[0])
    load_ahead = pltpu.make_async_copy(couplings.at[0], raw.at[0], load_sem.at[1])
    load_behind = pltpu.make_async_copy(couplings.at[1], raw.at[1], load_sem.at[2])
    load_sources = pltpu.make_async_copy(sources_hbm, sources, load_sem.at[4])
    load_sources.start()
    load_ahead.start()
    load_factor.start()
    load_behind.start()

    barrier = pltpu.get_barrier_semaphore()

    def greet(depth_index, lat):
        pl.semaphore_signal(barrier, inc=1, device_id=(depth_index, lat), device_id_type=MESH)

    greet(depth, other)

    @pl.when(place > 0)
    def _():
        greet(depth - 1, half)
        greet(depth - 1, other)

    @pl.when(place < SEG - 1)
    def _():
        greet(depth + 1, half)
        greet(depth + 1, other)

    for one, two in GREETS:
        @pl.when(place == one)
        def _():
            greet(depth + (two - one), half)

        @pl.when(place == two)
        def _():
            greet(depth - (two - one), half)

    at_edge = jnp.logical_or(place == 0, place == SEG - 1)
    callers = jnp.where(at_edge, 3, 5)
    for pair in GREETS:
        callers = callers + jnp.where(any_of(place, pair), 1, 0)

    load_sources.wait()
    load_ahead.wait()

    @pl.when(place == 0)
    def _():
        for row in range(HALF):
            reduced[base + row] = sources[:, row * BLK:(row + 1) * BLK].astype(BF16)

    @pl.when(place > 0)
    def _():
        split_couplings(raw.at[0], diag_ahead, side_ahead, base)
        for row in range(HALF):
            rounded[row] = sources[:, row * BLK:(row + 1) * BLK].astype(BF16)

    pl.semaphore_wait(barrier, callers)

    def tell(table):
        for one, two, slot in table:
            @pl.when(place == one)
            def _():
                pl.semaphore_signal(
                    go.at[slot], inc=1, device_id=(depth + (two - one), half), device_id_type=MESH
                )

    def wait_told(slot, among):
        places = [two for _, two, kind in TOLD if kind == slot and two in among]

        @pl.when(any_of(place, places))
        def _():
            pl.semaphore_wait(go.at[slot], 1)

    def once(source, target, slot, step, lat):
        return pltpu.make_async_remote_copy(
            src_ref=source, dst_ref=target, send_sem=once_send.at[slot], recv_sem=once_recv.at[slot],
            device_id=(depth + step, lat), device_id_type=MESH,
        )

    mine = pl.ds(base, HALF)
    theirs = pl.ds(their_base, HALF)
    swaps_ahead = any_of(place, SWAP_AHEAD)
    swaps_behind = any_of(place, SWAP_BEHIND)
    ahead_swaps = any_of(place + 1, SWAP_AHEAD)
    behind_swaps = any_of(place - 1, SWAP_BEHIND)
    give_reduced = once(reduced.at[mine], reduced.at[mine], 0, 0, other)
    take_reduced = once(reduced.at[theirs], reduced.at[theirs], 0, 0, other)
    give_pulled = once(pulled.at[mine], pulled.at[mine], 7, 0, other)
    take_pulled = once(pulled.at[theirs], pulled.at[theirs], 7, 0, other)
    give_pattern = once(pattern, their_pattern, 1, 0, other)
    give_source = once(rounded, source_next, 2, -1, half)
    give_diag_ahead = once(diag_ahead, diag_next, 3, -1, half)
    give_diag_behind = once(diag_behind, diag_prior, 4, 1, half)

    def side_copy(blocks, kind, owner, first, rows):
        part = blocks.at[pl.ds(owner * HALF + first, rows)]
        return once(part, part, 5 + kind, 0, other)

    def give_side(blocks, kind, paces, places, first=lambda: None):
        for pace in sorted(set(paces[p] for p in places if paces[p])):
            group = [p for p in places if paces[p] == pace]

            @pl.when(any_of(place, group))
            def _():
                wait_told(kind, group)
                first()

                def part(step, carry):
                    copy = side_copy(blocks, kind, half, step * pace, pace)
                    copy.start()
                    copy.wait_send()
                    return carry

                lax.fori_loop(0, HALF // pace, part, 0)

    def take_side(blocks, kind):
        side_copy(blocks, kind, other, 0, HALF).wait_recv()

    def chunk_copy(source, target, chunk, kind, owner, step, send, recv):
        return pltpu.make_async_remote_copy(
            src_ref=source.at[kind // 2, pl.ds(chunk * ROWS, ROWS)],
            dst_ref=target.at[pl.ds(owner * HALF + chunk * ROWS, ROWS)],
            send_sem=send.at[kind, chunk], recv_sem=recv.at[kind, chunk],
            device_id=(depth + step, other if kind else half), device_id_type=MESH,
        )

    def forward_copy(chunk, kind, owner):
        return chunk_copy(out_fwd, incoming_plus if kind == 2 else incoming, chunk, kind, owner, 1, fwd_send, fwd_recv)

    def backward_copy(chunk, kind, owner):
        return chunk_copy(out_bwd, later_plus if kind == 2 else later, chunk, kind, owner, -1, bwd_send, bwd_recv)

    def wait_arrivals(make, kinds):
        for kind in kinds:
            for chunk in range(CHUNKS):
                make(chunk, kind, other if kind else half).wait_recv()

    def wait_sent(make, swaps):
        for kind in (0, 1):
            for chunk in range(CHUNKS):
                make(chunk, kind, half).wait_send()

        @pl.when(jnp.logical_not(swaps))
        def _():
            for chunk in range(CHUNKS):
                make(chunk, 2, half).wait_send()

    def in_chunks(make, out, compute, ahead_of, swaps):
        for chunk in range(CHUNKS + 1):
            if chunk < CHUNKS:
                for row in range(chunk * ROWS, (chunk + 1) * ROWS):
                    out[0, row] = compute(row).astype(BF16)
                make(chunk, 1, half).start()
                make(chunk, 0, half).start()
            if chunk > 0:
                for row in range((chunk - 1) * ROWS, chunk * ROWS):
                    out[1, row] = ahead_of(out[0, row], row).astype(BF16)

                @pl.when(jnp.logical_not(swaps))
                def _():
                    make(chunk - 1, 2, half).start()

    def next_source(sent, row):
        return source_next[row] - dot(sent, diag_next[row])

    def prior_pulled(sent, row):
        return dot(sent, diag_prior[row])

    @pl.when(place == 0)
    def _():
        give_reduced.start()
        give_reduced.wait_send()

    tell(AFTER_START)
    give_pattern.start()

    @pl.when(jnp.logical_and(place > 0, jnp.logical_not(swaps_ahead)))
    def _():
        give_source.start()
        give_diag_ahead.start()

    give_side(side_ahead, AHEAD, PACE_AHEAD, FIRST_AHEAD)

    load_behind.wait()

    def take_diag_prior():
        @pl.when(jnp.logical_not(behind_swaps))
        def _():
            give_diag_behind.wait_recv()

    def prepare_behind():
        split_couplings(raw.at[1], diag_behind, side_behind, base)

    def start_diag_behind():
        @pl.when(jnp.logical_not(swaps_behind))
        def _():
            give_diag_behind.start()

    @pl.when(place < SEG - 1)
    def _():
        prepare_behind()

        @pl.when(lax.rem(place, 2) == 0)
        def _():
            start_diag_behind()

    give_side(side_behind, BEHIND, PACE_BEHIND, FIRST_BEHIND)
    load_factor.wait()
    transpose_factor(factor)

    give_side(side_ahead, AHEAD, PACE_AHEAD, [p for p in range(1, SEG) if p not in FIRST_AHEAD])
    give_pattern.wait_recv()
    load_cols = pltpu.make_async_copy(their_pattern, their_cols, load_sem.at[3])
    load_cols.start()
    load_cols.wait()

    @pl.when(place == 0)
    def _():
        take_reduced.wait_recv()

    def forward_row(row):
        value = row_apply(factor, reduced, cols, row)
        field[row] = value
        return value

    def last_row(row):
        value = row_apply(factor, reduced, cols, row)
        swept[:, row * BLK:(row + 1) * BLK] = value
        return value

    def backward_row(row):
        value = field[row] - row_apply(factor, pulled, cols, row)
        swept[:, row * BLK:(row + 1) * BLK] = value
        return value

    @pl.when(place > 0)
    def _():
        wait_arrivals(forward_copy, (0,))
        for row in range(HALF):
            near = dot(incoming[base + row], diag_ahead[row])
            partial[row] = sources[:, row * BLK:(row + 1) * BLK] - near
        wait_arrivals(forward_copy, (1,))
        for row in range(HALF):
            beside = dot(incoming[cols[1, row]], side_ahead[base + row])
            reduced[base + row] = (partial[row] - beside).astype(BF16)

        @pl.when(swaps_ahead)
        def _():
            give_reduced.start()
            take_reduced.wait_recv()

        @pl.when(jnp.logical_not(swaps_ahead))
        def _():
            take_side(side_ahead, AHEAD)
            wait_arrivals(forward_copy, (2,))
            for row in range(HALF):
                beside = dot(incoming[their_cols[1, row]], side_ahead[their_base + row])
                reduced[their_base + row] = (incoming_plus[their_base + row] - beside).astype(BF16)

    @pl.when(jnp.logical_and(place < SEG - 1, jnp.logical_not(ahead_swaps)))
    def _():
        give_source.wait_recv()
        give_diag_ahead.wait_recv()

    @pl.when(place == SEG - 1)
    def _():
        take_diag_prior()
        in_chunks(backward_copy, out_bwd, last_row, prior_pulled, behind_swaps)

    @pl.when(place < SEG - 1)
    def _():
        in_chunks(forward_copy, out_fwd, forward_row, next_source, ahead_swaps)

    tell(AT_FORWARD)

    @pl.when(place == 3)
    def _():
        start_diag_behind()

    def start_diag_far():
        @pl.when(any_of(place, (1, 5)))
        def _():
            start_diag_behind()


    rest = [p for p in range(SEG - 1) if p not in FIRST_BEHIND]
    give_side(side_behind, BEHIND, PACE_BEHIND, rest, start_diag_far)

    @pl.when(place < SEG - 1)
    def _():
        wait_sent(forward_copy, ahead_swaps)

    @pl.when(place < SEG - 1)
    def _():
        wait_arrivals(backward_copy, (0,))
        for row in range(HALF):
            partial[row] = dot(later[base + row], diag_behind[row])
        wait_arrivals(backward_copy, (1,))
        for row in range(HALF):
            beside = dot(later[cols[1, row]], side_behind[base + row])
            pulled[base + row] = (partial[row] + beside).astype(BF16)

        @pl.when(swaps_behind)
        def _():
            give_pulled.start()
            take_pulled.wait_recv()

        @pl.when(jnp.logical_not(swaps_behind))
        def _():
            take_side(side_behind, BEHIND)
            wait_arrivals(backward_copy, (2,))
            for row in range(HALF):
                beside = dot(later[their_cols[1, row]], side_behind[their_base + row])
                pulled[their_base + row] = (later_plus[their_base + row] + beside).astype(BF16)

        @pl.when(place > 0)
        def _():
            take_diag_prior()
            in_chunks(backward_copy, out_bwd, backward_row, prior_pulled, behind_swaps)

        @pl.when(place == 0)
        def _():
            for row in range(HALF):
                backward_row(row)


    tell(AT_BACKWARD)

    @pl.when(place > 0)
    def _():
        wait_sent(backward_copy, behind_swaps)

    @pl.when(swaps_ahead)
    def _():
        give_reduced.wait_send()

    @pl.when(swaps_behind)
    def _():
        give_pulled.wait_send()

    give_pattern.wait_send()

    @pl.when(jnp.logical_and(place > 0, jnp.logical_not(swaps_ahead)))
    def _():
        give_source.wait_send()
        give_diag_ahead.wait_send()

    @pl.when(jnp.logical_and(place < SEG - 1, jnp.logical_not(swaps_behind)))
    def _():
        give_diag_behind.wait_send()


def local(sources, frontal, couplings, pattern):
    vector = pltpu.VMEM((NBR, SHOTS, BLK), BF16)
    half_vector = pltpu.VMEM((HALF, SHOTS, BLK), BF16)
    half_double = pltpu.VMEM((2, HALF, SHOTS, BLK), BF16)
    half_blocks = pltpu.VMEM((HALF, BLK, BLK), BF16)
    blocks = pltpu.VMEM((NBR, BLK, BLK), BF16)
    vmem = pl.BlockSpec(memory_space=pltpu.VMEM)
    hbm = pl.BlockSpec(memory_space=pl.ANY)
    smem = pl.BlockSpec(memory_space=pltpu.SMEM)
    chunk_sem = pltpu.SemaphoreType.DMA((3, CHUNKS))
    columns = pattern[0].T
    once_sem = pltpu.SemaphoreType.DMA((8,))
    out = pl.pallas_call(
        sweep_kernel,
        out_shape=jax.ShapeDtypeStruct((SHOTS, HALF * BLK), F32),
        in_specs=[hbm, hbm, hbm, hbm, smem],
        out_specs=vmem,
        scratch_shapes=[
            pltpu.VMEM((SHOTS, HALF * BLK), F32),
            pltpu.VMEM((HALF, SHOTS, BLK), F32),
            pltpu.VMEM((HALF, KH, BLK, BLK), BF16),
            pltpu.VMEM((2, HALF, KC, BLK, BLK), BF16),
            half_blocks, half_blocks, blocks, blocks, half_blocks, half_blocks,
            half_vector, half_vector,
            pltpu.VMEM((KH, HALF), jnp.int32),
            pltpu.SMEM((KH, HALF), jnp.int32),
            pltpu.VMEM((HALF, SHOTS, BLK), F32),
            vector, vector, vector, vector, vector, vector, half_double, half_double,
            pltpu.SemaphoreType.DMA((5,)),
            once_sem, once_sem, chunk_sem, chunk_sem, chunk_sem, chunk_sem,
            pltpu.SemaphoreType.REGULAR((2,)),
        ],
        compiler_params=pltpu.CompilerParams(
            collective_id=0, has_side_effects=True, vmem_limit_bytes=60 * 1024 * 1024
        ),
    )(sources[0], frontal[0], couplings[0], columns, columns)
    return out[None]


def solution(mesh):
    return jax.shard_map(
        local,
        mesh=mesh,
        in_specs=(
            P("depth", None, "lat"),
            P("depth", "lat", None, None, None),
            P("depth", None, "lat", None, None, None),
            P("depth", "lat", None),
        ),
        out_specs=P("depth", None, "lat"),
        check_vma=False,
    )
```

time: 172 us -> 141 us (0.82)
  Pallas kernels: 168 us -> 139 us
  local copies, waits for them, and re-layouts: 4.25 us -> 1.62 us
    pallas_call x1, Pallas kernels: 168 us -> 139 us  [local(): pl.pallas_call(sweep_kernel, out_shape=jax.ShapeDtypeStruct((SHOTS, HALF...]
    unnamed x6 -> x1, local copies, waits for them, and re-layouts: 4.25 us -> 1.62 us
where the time goes in v2:
time: 141 us
  Pallas kernels  139 us (99%)
  local copies, waits for them, and re-layouts  1.62 us (1%)
    pallas_call x1, Pallas kernels, local(): pl.pallas_call(sweep_kernel, out_shape=jax.ShapeDtypeStruct((SHOTS, HALF...  139 us

profile of v2, /device:TPU:4, one launch (start us, length us, event | category | flops | bytes accessed | tf_op | source)
XLA Modules:
  0.0 140.8 jit_solution(10935066054259429496)
XLA Ops:
  0.0 139.1 %shard_map.46 = f32[16,3072]{1,0:T(8,128)} custom-call(f32[16,3072]{1,0:T(8,128)} %bitcast.10, bf16[24,8,128,128]{3,2,1,0:T(8,128)(2,1)} %bitcast.7, bf16[2,24,2,128,128]{4,3,2,1,0:T(8,128)(2,1)} %bitcast.8, s32[8,24]{1,0:T(8,128)} %bitcast.11, s32[8,24]{1,0:T(8,128)} %bitcast.12), custom_call_target="tpu_custom_call" | custom-call | tf_op jit(solution)/shard_map/pallas_call | solution.py:452
  139.1 1.6 %copy.6 = f32[1,16,3072]{2,1,0:T(8,128)} copy(f32[1,16,3072]{2,1,0:T(8,128)} %bitcast.9) | data formatting | bytes 393216

commit v3 on v2

--- a/solution.py
+++ b/solution.py
@@ -13,22 +13,21 @@
 SHOTS = 16
 NBR = 48
 HALF = 24
-CHUNKS = 4
+CHUNKS = 3
 ROWS = HALF // CHUNKS
 F32 = jnp.float32
 BF16 = jnp.bfloat16
 NN = (((1,), (0,)), ((), ()))
 
 SWAP_AHEAD = (2,)
-SWAP_BEHIND = ()
+SWAP_BEHIND = (6,)
 AHEAD, BEHIND = range(2)
 AFTER_START = ()
-AT_FORWARD = ((0, 4, AHEAD), (1, 5, AHEAD), (1, 6, AHEAD), (2, 7, AHEAD), (6, 1, BEHIND))
-AT_BACKWARD = ((6, 2, BEHIND),)
-PACE_AHEAD = (0, 24, 0, 24, 2, 2, 2, 2)
-PACE_BEHIND = (12, 3, 4, 12, 3, 4, 24, 0)
-FIRST_AHEAD = (1, 3)
-FIRST_BEHIND = (6,)
+AT_FORWARD = ((0, 4, AHEAD), (1, 5, AHEAD), (3, 7, AHEAD), (7, 1, BEHIND))
+AT_BACKWARD = ((6, 2, BEHIND), (6, 3, BEHIND))
+PACE_AHEAD = (0, 24, 0, 24, 2, 2, 24, 4)
+PACE_BEHIND = (4, 4, 4, 8, 3, 4, 0, 0)
+FIRST_AHEAD = (1, 3, 6)
 PACES = (PACE_AHEAD, PACE_BEHIND)
 AFTER_START = tuple(told for told in AFTER_START if PACES[told[2]][told[1]])
 AT_FORWARD = tuple(told for told in AT_FORWARD if PACES[told[2]][told[1]])
@@ -76,7 +75,7 @@
 
 def sweep_kernel(
     sources_hbm, frontal, couplings, pattern, cols, swept,
-    sources, partial, factor, raw, diag_ahead, diag_behind, side_ahead, side_behind, diag_next, diag_prior,
+    sources, partial, theirs_part, factor, raw, diag_ahead, diag_behind, side_ahead, side_behind, diag_next, diag_prior,
     rounded, source_next, their_pattern, their_cols, field, incoming, later, incoming_plus, later_plus, reduced, pulled, out_fwd, out_bwd,
     load_sem, once_send, once_recv, fwd_send, fwd_recv, bwd_send, bwd_recv, go,
 ):
@@ -291,7 +290,6 @@
         def _():
             start_diag_behind()
 
-    give_side(side_behind, BEHIND, PACE_BEHIND, FIRST_BEHIND)
     load_factor.wait()
     transpose_factor(factor)
 
@@ -339,10 +337,11 @@
         @pl.when(jnp.logical_not(swaps_ahead))
         def _():
             take_side(side_ahead, AHEAD)
+            for row in range(HALF):
+                theirs_part[row] = dot(incoming[their_cols[1, row]], side_ahead[their_base + row])
             wait_arrivals(forward_copy, (2,))
             for row in range(HALF):
-                beside = dot(incoming[their_cols[1, row]], side_ahead[their_base + row])
-                reduced[their_base + row] = (incoming_plus[their_base + row] - beside).astype(BF16)
+                reduced[their_base + row] = (incoming_plus[their_base + row] - theirs_part[row]).astype(BF16)
 
     @pl.when(jnp.logical_and(place < SEG - 1, jnp.logical_not(ahead_swaps)))
     def _():
@@ -370,8 +369,7 @@
             start_diag_behind()
 
 
-    rest = [p for p in range(SEG - 1) if p not in FIRST_BEHIND]
-    give_side(side_behind, BEHIND, PACE_BEHIND, rest, start_diag_far)
+    give_side(side_behind, BEHIND, PACE_BEHIND, range(SEG - 1), start_diag_far)
 
     @pl.when(place < SEG - 1)
     def _():
@@ -395,10 +393,11 @@
         @pl.when(jnp.logical_not(swaps_behind))
         def _():
             take_side(side_behind, BEHIND)
+            for row in range(HALF):
+                theirs_part[row] = dot(later[their_cols[1, row]], side_behind[their_base + row])
             wait_arrivals(backward_copy, (2,))
             for row in range(HALF):
-                beside = dot(later[their_cols[1, row]], side_behind[their_base + row])
-                pulled[their_base + row] = (later_plus[their_base + row] + beside).astype(BF16)
+                pulled[their_base + row] = (later_plus[their_base + row] + theirs_part[row]).astype(BF16)
 
         @pl.when(place > 0)
         def _():
@@ -457,6 +456,7 @@
         scratch_shapes=[
             pltpu.VMEM((SHOTS, HALF * BLK), F32),
             pltpu.VMEM((HALF, SHOTS, BLK), F32),
+            pltpu.VMEM((HALF, SHOTS, BLK), F32),
             pltpu.VMEM((HALF, KH, BLK, BLK), BF16),
             pltpu.VMEM((2, HALF, KC, BLK, BLK), BF16),
             half_blocks, half_blocks, blocks, blocks, half_blocks, half_blocks,

time: 141 us -> 135 us (0.957)
  Pallas kernels: 139 us -> 133 us
    pallas_call x1, Pallas kernels: 139 us -> 133 us  [local(): pl.pallas_call(sweep_kernel, out_shape=jax.ShapeDtypeStruct((SHOTS, HALF...]
where the time goes in v3:
time: 135 us
  Pallas kernels  133 us (99%)
  local copies, waits for them, and re-layouts  1.62 us (1%)
    pallas_call x1, Pallas kernels, local(): pl.pallas_call(sweep_kernel, out_shape=jax.ShapeDtypeStruct((SHOTS, HALF...  133 us

profile of v3, /device:TPU:4, one launch (start us, length us, event | category | flops | bytes accessed | tf_op | source)
XLA Modules:
  0.0 134.5 jit_solution(3425978073746476863)
XLA Ops:
  0.0 132.9 %shard_map.46 = f32[16,3072]{1,0:T(8,128)} custom-call(f32[16,3072]{1,0:T(8,128)} %bitcast.10, bf16[24,8,128,128]{3,2,1,0:T(8,128)(2,1)} %bitcast.7, bf16[2,24,2,128,128]{4,3,2,1,0:T(8,128)(2,1)} %bitcast.8, s32[8,24]{1,0:T(8,128)} %bitcast.11, s32[8,24]{1,0:T(8,128)} %bitcast.12), custom_call_target="tpu_custom_call" | custom-call | tf_op jit(solution)/shard_map/pallas_call | solution.py:451
  132.9 1.6 %copy.6 = f32[1,16,3072]{2,1,0:T(8,128)} copy(f32[1,16,3072]{2,1,0:T(8,128)} %bitcast.9) | data formatting | bytes 393216

commit v4 on v3

--- a/solution.py
+++ b/solution.py
@@ -23,10 +23,10 @@
 SWAP_BEHIND = (6,)
 AHEAD, BEHIND = range(2)
 AFTER_START = ()
-AT_FORWARD = ((0, 4, AHEAD), (1, 5, AHEAD), (3, 7, AHEAD), (7, 1, BEHIND))
-AT_BACKWARD = ((6, 2, BEHIND), (6, 3, BEHIND))
-PACE_AHEAD = (0, 24, 0, 24, 2, 2, 24, 4)
-PACE_BEHIND = (4, 4, 4, 8, 3, 4, 0, 0)
+AT_FORWARD = ((0, 4, AHEAD), (1, 5, AHEAD), (3, 7, AHEAD))
+AT_BACKWARD = ((6, 2, BEHIND), (6, 3, BEHIND), (4, 1, BEHIND))
+PACE_AHEAD = (0, 24, 0, 24, 4, 3, 12, 8)
+PACE_BEHIND = (4, 24, 4, 8, 3, 4, 0, 0)
 FIRST_AHEAD = (1, 3, 6)
 PACES = (PACE_AHEAD, PACE_BEHIND)
 AFTER_START = tuple(told for told in AFTER_START if PACES[told[2]][told[1]])
@@ -182,14 +182,13 @@
         part = blocks.at[pl.ds(owner * HALF + first, rows)]
         return once(part, part, 5 + kind, 0, other)
 
-    def give_side(blocks, kind, paces, places, first=lambda: None):
+    def give_side(blocks, kind, paces, places):
         for pace in sorted(set(paces[p] for p in places if paces[p])):
             group = [p for p in places if paces[p] == pace]
 
             @pl.when(any_of(place, group))
             def _():
                 wait_told(kind, group)
-                first()
 
                 def part(step, carry):
                     copy = side_copy(blocks, kind, half, step * pace, pace)
@@ -359,21 +358,15 @@
 
     tell(AT_FORWARD)
 
-    @pl.when(place == 3)
-    def _():
-        start_diag_behind()
-
-    def start_diag_far():
-        @pl.when(any_of(place, (1, 5)))
+    @pl.when(place < SEG - 1)
+    def _():
+        wait_sent(forward_copy, ahead_swaps)
+
+        @pl.when(lax.rem(place, 2) == 1)
         def _():
             start_diag_behind()
 
-
-    give_side(side_behind, BEHIND, PACE_BEHIND, range(SEG - 1), start_diag_far)
-
-    @pl.when(place < SEG - 1)
-    def _():
-        wait_sent(forward_copy, ahead_swaps)
+    give_side(side_behind, BEHIND, PACE_BEHIND, range(SEG - 1))
 
     @pl.when(place < SEG - 1)
     def _():

time: 135 us -> 130 us (0.963)
  Pallas kernels: 133 us -> 128 us
    pallas_call x1, Pallas kernels: 133 us -> 128 us  [local(): pl.pallas_call(sweep_kernel, out_shape=jax.ShapeDtypeStruct((SHOTS, HALF...]
where the time goes in v4:
time: 130 us
  Pallas kernels  128 us (98%)
  local copies, waits for them, and re-layouts  1.62 us (1%)
    pallas_call x1, Pallas kernels, local(): pl.pallas_call(sweep_kernel, out_shape=jax.ShapeDtypeStruct((SHOTS, HALF...  128 us

profile of v4, /device:TPU:4, one launch (start us, length us, event | category | flops | bytes accessed | tf_op | source)
XLA Modules:
  0.0 129.9 jit_solution(8639940812145566828)
XLA Ops:
  0.0 128.3 %shard_map.46 = f32[16,3072]{1,0:T(8,128)} custom-call(f32[16,3072]{1,0:T(8,128)} %bitcast.10, bf16[24,8,128,128]{3,2,1,0:T(8,128)(2,1)} %bitcast.7, bf16[2,24,2,128,128]{4,3,2,1,0:T(8,128)(2,1)} %bitcast.8, s32[8,24]{1,0:T(8,128)} %bitcast.11, s32[8,24]{1,0:T(8,128)} %bitcast.12), custom_call_target="tpu_custom_call" | custom-call | tf_op jit(solution)/shard_map/pallas_call | solution.py:444
  128.3 1.6 %copy.6 = f32[1,16,3072]{2,1,0:T(8,128)} copy(f32[1,16,3072]{2,1,0:T(8,128)} %bitcast.9) | data formatting | bytes 393216

commit v5 on v4

--- a/solution.py
+++ b/solution.py
@@ -24,9 +24,9 @@
 AHEAD, BEHIND = range(2)
 AFTER_START = ()
 AT_FORWARD = ((0, 4, AHEAD), (1, 5, AHEAD), (3, 7, AHEAD))
-AT_BACKWARD = ((6, 2, BEHIND), (6, 3, BEHIND), (4, 1, BEHIND))
+AT_BACKWARD = ((6, 3, BEHIND), (5, 2, BEHIND), (4, 1, BEHIND))
 PACE_AHEAD = (0, 24, 0, 24, 4, 3, 12, 8)
-PACE_BEHIND = (4, 24, 4, 8, 3, 4, 0, 0)
+PACE_BEHIND = (4, 24, 8, 8, 3, 4, 0, 0)
 FIRST_AHEAD = (1, 3, 6)
 PACES = (PACE_AHEAD, PACE_BEHIND)
 AFTER_START = tuple(told for told in AFTER_START if PACES[told[2]][told[1]])

time: 130 us -> 130 us (level)
  no operation moved by 1% of the time
where the time goes in v5:
time: 130 us; the launch traced here: 129 us
  Pallas kernels  128 us (98%)
  local copies, waits for them, and re-layouts  1.62 us (1%)
    pallas_call x1, Pallas kernels, local(): pl.pallas_call(sweep_kernel, out_shape=jax.ShapeDtypeStruct((SHOTS, HALF...  128 us

profile of v5, /device:TPU:4, one launch (start us, length us, event | category | flops | bytes accessed | tf_op | source)
XLA Modules:
  0.0 129.3 jit_solution(16977856983855130470)
XLA Ops:
  0.0 127.7 %shard_map.46 = f32[16,3072]{1,0:T(8,128)} custom-call(f32[16,3072]{1,0:T(8,128)} %bitcast.10, bf16[24,8,128,128]{3,2,1,0:T(8,128)(2,1)} %bitcast.7, bf16[2,24,2,128,128]{4,3,2,1,0:T(8,128)(2,1)} %bitcast.8, s32[8,24]{1,0:T(8,128)} %bitcast.11, s32[8,24]{1,0:T(8,128)} %bitcast.12), custom_call_target="tpu_custom_call" | custom-call | tf_op jit(solution)/shard_map/pallas_call | solution.py:444
  127.7 1.6 %copy.6 = f32[1,16,3072]{2,1,0:T(8,128)} copy(f32[1,16,3072]{2,1,0:T(8,128)} %bitcast.9) | data formatting | bytes 393216

commit v6 on v5

--- a/solution.py
+++ b/solution.py
@@ -25,7 +25,7 @@
 AFTER_START = ()
 AT_FORWARD = ((0, 4, AHEAD), (1, 5, AHEAD), (3, 7, AHEAD))
 AT_BACKWARD = ((6, 3, BEHIND), (5, 2, BEHIND), (4, 1, BEHIND))
-PACE_AHEAD = (0, 24, 0, 24, 4, 3, 12, 8)
+PACE_AHEAD = (0, 24, 0, 24, 4, 3, 12, 6)
 PACE_BEHIND = (4, 24, 8, 8, 3, 4, 0, 0)
 FIRST_AHEAD = (1, 3, 6)
 PACES = (PACE_AHEAD, PACE_BEHIND)

time: 130 us -> 130 us (level)
  no operation moved by 1% of the time
where the time goes in v6:
time: 130 us; the launch traced here: 129 us
  Pallas kernels  128 us (98%)
  local copies, waits for them, and re-layouts  1.62 us (1%)
    pallas_call x1, Pallas kernels, local(): pl.pallas_call(sweep_kernel, out_shape=jax.ShapeDtypeStruct((SHOTS, HALF...  128 us

profile of v6, /device:TPU:4, one launch (start us, length us, event | category | flops | bytes accessed | tf_op | source)
XLA Modules:
  0.0 129.4 jit_solution(242959314282412795)
XLA Ops:
  0.0 127.7 %shard_map.46 = f32[16,3072]{1,0:T(8,128)} custom-call(f32[16,3072]{1,0:T(8,128)} %bitcast.10, bf16[24,8,128,128]{3,2,1,0:T(8,128)(2,1)} %bitcast.7, bf16[2,24,2,128,128]{4,3,2,1,0:T(8,128)(2,1)} %bitcast.8, s32[8,24]{1,0:T(8,128)} %bitcast.11, s32[8,24]{1,0:T(8,128)} %bitcast.12), custom_call_target="tpu_custom_call" | custom-call | tf_op jit(solution)/shard_map/pallas_call | solution.py:444
  127.8 1.6 %copy.6 = f32[1,16,3072]{2,1,0:T(8,128)} copy(f32[1,16,3072]{2,1,0:T(8,128)} %bitcast.9) | data formatting | bytes 393216
